TPU v7x, 768 devices: a whole 4x8x12 slice. The times are simulated.
768 devices in a mesh: grp: 16 (over y, core), rep: 48 (over x, z).
Axes of the slice: x: 4, y: 8, z: 12, core: 2. Of those that a mesh axis runs over, the one named last changes fastest.
Arguments:
- grad_part: float32 [16, 3072, 20, 512], P('grp', 'rep'), may hold values from -0.75 to 0.75
- owners: int32 [6, 20], replicated, may hold values from 0 to 47, as said below
- readers: int32 [48], replicated, may hold values from 0 to 47, each once
- left_stat: float32 [48, 4, 512, 512], P('rep', None, 'grp'), may hold values from -6 to 6
- right_stat: float32 [48, 4, 512, 512], P('rep', None, 'grp'), may hold values from -6 to 6
- left_root: bfloat16 [48, 4, 512, 512], P('rep'), may hold values from -1 to 2
- right_root: bfloat16 [48, 4, 512, 512], P('rep', None, None, 'grp'), may hold values from -1 to 2
Outputs:
- update: bfloat16 [3072, 20, 512], P('rep', None, 'grp')
- left_new: float32 [48, 4, 512, 512], P('rep', None, 'grp')
- right_new: float32 [48, 4, 512, 512], P('rep', None, 'grp')
Inputs may be any that keep to these rules, and one draw needn't show every extreme that they name: `owners`: A device owns at most 1 block of one block row and at most 4 blocks in all; some device owns 4 blocks.
All inputs are finite; a program needn't handle non-finite values.
Results may differ from a plain program's by a relative error of at most 0.0057.
Values may be sent and summed in bfloat16 or wider, within the bound.
A program may use at most 64 MiB of HBM per device.

v0:
```python
import jax
import jax.numpy as jnp
from jax import lax
from jax.sharding import PartitionSpec as P

decay = 0.95


def make_absorb(owned_cols, right_cols, top_start, strip_width):

    def absorb(carry, piece, start):
        top_rows = lax.dynamic_slice_in_dim(piece, top_start, strip_width, 1)
        left_acc = jnp.einsum("sai,sbi->sab", top_rows, piece, preferred_element_type=jnp.float32)
        right_term = jnp.einsum(
            "sia,sib->sab", owned_cols, piece, preferred_element_type=jnp.float32
        )
        mixed_acc = jnp.einsum(
            "sai,sic->sac", piece, right_cols, preferred_element_type=jnp.float32
        )
        return (left_acc, right_term, mixed_acc)

    return absorb


def empty_sums(count_now, block_size, strip_width):
    return (
        jnp.zeros((count_now, strip_width, block_size), jnp.float32),
        jnp.zeros((count_now, strip_width, block_size), jnp.float32),
        jnp.zeros((count_now, block_size, strip_width), jnp.float32),
    )


def on_device(grad_part, owners, readers, left_stat, right_stat, left_root, right_root):
    group_count = lax.axis_size("grp")
    peer_count = lax.axis_size("rep")
    my_group = lax.axis_index("grp")
    my_peer = lax.axis_index("rep")
    shard_rows = grad_part.shape[1]
    block_cols = grad_part.shape[2]
    block_size = grad_part.shape[3]
    strip_width = block_size // group_count
    slot_count = left_stat.shape[1]
    lane_count = -(-block_cols // peer_count)
    per_block = block_size // shard_rows
    owners_flat = owners.reshape(-1)
    block_total = owners_flat.shape[0]
    block_index = jnp.arange(block_total, dtype=jnp.int32)
    block_row = block_index // block_cols
    earlier = block_index[None, :] < block_index[:, None]
    same_owner = owners_flat[:, None] == owners_flat[None, :]
    owner_slot = jnp.sum((same_owner & earlier).astype(jnp.int32), axis=1)
    same_row = block_row[:, None] == block_row[None, :]
    row_rank = jnp.sum((same_owner & earlier & same_row).astype(jnp.int32), axis=1)
    peer_ids = jnp.arange(peer_count, dtype=jnp.int32)
    lane_ids = jnp.arange(lane_count, dtype=jnp.int32)
    summed = lax.psum_scatter(grad_part[0], "grp", scatter_dimension=2, tiled=True)
    pieces = summed.astype(jnp.bfloat16)
    my_row = my_peer * shard_rows // block_size
    targets = lax.dynamic_slice_in_dim(owners_flat, my_row * block_cols, block_cols)
    target_lane = lax.dynamic_slice_in_dim(row_rank, my_row * block_cols, block_cols)
    routing = (
        (peer_ids[:, None, None] == targets[None, None, :])
        & (lane_ids[None, :, None] == target_lane[None, None, :])
    ).astype(jnp.bfloat16)
    outgoing = jnp.einsum(
        "pcj,tjh->pcth", routing, pieces, preferred_element_type=jnp.float32
    ).astype(jnp.bfloat16)
    arrived = lax.all_to_all(outgoing, "rep", split_axis=0, concat_axis=0, tiled=True)
    slot_ids = jnp.arange(slot_count, dtype=jnp.int32)
    slot_hit = (
        (owners_flat[None, :] == my_peer) & (owner_slot[None, :] == slot_ids[:, None])
    ).astype(jnp.int32)
    filled = jnp.sum(slot_hit, axis=1) > 0
    slot_row = jnp.sum(slot_hit * block_row[None, :], axis=1)
    slot_lane = jnp.sum(slot_hit * row_rank[None, :], axis=1)
    part_ids = jnp.arange(per_block, dtype=jnp.int32)
    source = slot_row[:, None] * per_block + part_ids[None, :]
    picking = (
        filled[:, None, None, None]
        & (source[:, :, None, None] == peer_ids[None, None, :, None])
        & (slot_lane[:, None, None, None] == lane_ids[None, None, None, :])
    ).astype(jnp.bfloat16)
    owned_cols = jnp.einsum("suqc,qcth->suth", picking, arrived, preferred_element_type=jnp.float32)
    owned_cols = owned_cols.astype(jnp.bfloat16).reshape(slot_count, block_size, strip_width)
    right_cols = right_root[0]
    top_start = my_group * strip_width
    left_parts = []
    right_parts = []
    mixed_parts = []
    for slot_num in range(slot_count):
        single = owned_cols[slot_num : slot_num + 1]
        absorb = make_absorb(single, right_cols[slot_num : slot_num + 1], top_start, strip_width)
        left_one, right_one, mixed_one = absorb(
            empty_sums(1, block_size, strip_width),
            lax.all_gather(single, "grp", axis=2, tiled=True),
            jnp.int32(0),
        )
        left_parts.append(left_one)
        right_parts.append(right_one)
        mixed_parts.append(mixed_one)
    left_acc = jnp.concatenate(left_parts, axis=0)
    right_acc = jnp.concatenate(right_parts, axis=0)
    mixed_acc = jnp.concatenate(mixed_parts, axis=0)
    left_next = decay * left_stat[0] + (1.0 - decay) * left_acc
    right_next = decay * right_stat[0] + (1.0 - decay) * right_acc
    mixed = mixed_acc.astype(jnp.bfloat16)
    result = jnp.einsum(
        "sab,sbc->sac", left_root[0], mixed, preferred_element_type=jnp.float32
    ).astype(jnp.bfloat16)
    shaped = result.reshape(slot_count, per_block, shard_rows, strip_width)
    reader_of = jnp.sum(
        (source[:, :, None] == peer_ids[None, None, :]).astype(jnp.int32) * readers[None, None, :],
        axis=2,
    )
    homeward_map = (
        (peer_ids[:, None, None, None] == reader_of[None, None, :, :])
        & (lane_ids[None, :, None, None] == slot_lane[None, None, :, None])
        & filled[None, None, :, None]
    ).astype(jnp.bfloat16)
    homeward = jnp.einsum(
        "pcsu,suth->pcth", homeward_map, shaped, preferred_element_type=jnp.float32
    ).astype(jnp.bfloat16)
    returned = lax.all_to_all(homeward, "rep", split_axis=0, concat_axis=0, tiled=True)
    my_source = jnp.sum(peer_ids * (readers == my_peer).astype(jnp.int32))
    source_row = my_source * shard_rows // block_size
    row_owners = lax.dynamic_slice_in_dim(owners_flat, source_row * block_cols, block_cols)
    row_lanes = lax.dynamic_slice_in_dim(row_rank, source_row * block_cols, block_cols)
    choose = (
        (row_owners[:, None, None] == peer_ids[None, :, None])
        & (row_lanes[:, None, None] == lane_ids[None, None, :])
    ).astype(jnp.bfloat16)
    update = jnp.einsum(
        "joc,octh->tjh", choose, returned, preferred_element_type=jnp.float32
    ).astype(jnp.bfloat16)
    return (update, left_next[None], right_next[None])


def solution(mesh):
    placed = (
        P("grp", "rep", None, None),
        P(),
        P(),
        P("rep", None, "grp", None),
        P("rep", None, "grp", None),
        P("rep", None, None, None),
        P("rep", None, None, "grp"),
    )
    return jax.shard_map(
        on_device,
        mesh=mesh,
        in_specs=placed,
        out_specs=(P("rep", None, "grp"), P("rep", None, "grp", None), P("rep", None, "grp", None)),
        check_vma=False,
    )
```

profile of v0, /device:TPU:1, one launch (start us, length us, event | category | flops | bytes accessed | tf_op | source)
XLA Modules:
  0.0 231.5 jit_solution(17070698162417540469)
XLA Ops:
  7.2 0.0 copy-start
  7.2 0.0 reduce-scatter.2.cloned.1.call-start
  7.2 5.5 %copy.20 = f32[1,64,20,512]{1,2,3,0:T(8,128)} copy(f32[1,64,20,512]{3,1,2,0:T(8,128)} %param.7) | data formatting | bytes 5242880 | tf_op args[0]
  12.7 0.0 reduce-scatter.2.cloned.1.call-update
  12.7 0.6 copy-done.12
  13.4 0.6 fusion.88
  14.7 0.1 broadcast_in_dim_reshape.2
  14.8 0.1 fusion.91
  14.9 0.2 convert_reduce_fusion.1
  15.1 0.7 dynamic-slice_compare_fusion
  15.7 0.2 convert_reduce_fusion.2
  15.9 74.9 %reduce-scatter.2.cloned.1.call-done = f32[64,20,32]{0,1,2:T(8,128)} async-done(((f32[64,20,512]{0,1,2:T(8,128)}), f32[64,20,32]{0,1,2:T(8,128)}) %reduce-scatter.2.cloned.1.call-update) | async-done | bytes 163856 | tf_op jit(solution)/shard_map/reduce_scatter | solution.py:56
  90.8 1.4 fusion.3
  92.1 0.1 copy.40
  92.2 0.0 copy-start.9
  92.3 0.9 reshape.432
  93.2 11.4 %all-to-all-start = ((bf16[48,2,1024]{2,1,0:T(2,128)(2,1)}), bf16[48,2,1024]{2,1,0:T(2,128)(2,1)S(1)}, u32[]{:S(2)}, u32[]{:S(2)}) async-start(bf16[48,2,1024]{2,1,0:T(2,128)(2,1)} %reshape.432), calls=%async_computation.1 | async-start | bytes 393216 | tf_op jit(solution)/shard_map/all_to_all | solution.py:68
  104.6 0.1 iota_add_fusion
  104.7 0.2 select_reduce_fusion
  104.9 12.6 %all-to-all-done = bf16[48,2,1024]{2,1,0:T(2,128)(2,1)S(1)} async-done(((bf16[48,2,1024]{2,1,0:T(2,128)(2,1)}), bf16[48,2,1024]{2,1,0:T(2,128)(2,1)S(1)}, u32[]{:S(2)}, u32[]{:S(2)}) %all-to-all-start) | async-done | bytes 196640 | tf_op jit(solution)/shard_map/all_to_all | solution.py:68
  117.5 0.3 reshape.433
  117.8 0.3 convolution_convert_fusion.1
  118.1 0.1 slice.50
  118.2 21.8 %all_gather.15 = bf16[1,512,512]{1,2,0:T(8,128)(2,1)S(1)} all-gather(bf16[1,512,32]{1,2,0:T(8,128)(2,1)S(1)} %slice.50), channel_id=1, replica_groups=mesh['grp'=16,'rep'=48] {'grp'}, dimensions={2}, use_global_device_ids=true | all-gather | bytes 557056 | tf_op jit(solution)/shard_map/all_gather | solution.py:95
  140.0 0.7 slice.47
  140.7 17.1 %all_gather.14 = bf16[1,512,512]{1,2,0:T(8,128)(2,1)S(1)} all-gather(bf16[1,512,32]{1,2,0:T(8,128)(2,1)} %slice.47), channel_id=1, replica_groups=mesh['grp'=16,'rep'=48] {'grp'}, dimensions={2}, use_global_device_ids=true | all-gather | bytes 557056 | tf_op jit(solution)/shard_map/all_gather | solution.py:95
  157.8 0.0 copy-done.9
  157.8 0.8 fusion.15
  158.6 0.8 fusion.14
  159.4 0.9 convolution_bitcast_fusion.1
  160.3 0.9 convolution_bitcast_fusion.2
  161.3 0.7 slice.44
  162.0 16.5 %all_gather.13 = bf16[1,512,512]{1,2,0:T(8,128)(2,1)S(1)} all-gather(bf16[1,512,32]{1,2,0:T(8,128)(2,1)} %slice.44), channel_id=1, replica_groups=mesh['grp'=16,'rep'=48] {'grp'}, dimensions={2}, use_global_device_ids=true | all-gather | bytes 557056 | tf_op jit(solution)/shard_map/all_gather | solution.py:95
  178.5 0.8 fusion.13
  179.3 0.9 convolution_bitcast_fusion.3
  180.2 0.7 reshape.425
  181.0 0.7 reshape.424
  181.7 0.7 reshape.423
  182.4 0.1 slice.41
  182.5 0.7 reshape.422
  183.2 16.8 %all_gather.12 = bf16[1,512,512]{1,2,0:T(8,128)(2,1)S(1)} all-gather(bf16[1,512,32]{1,2,0:T(8,128)(2,1)S(1)} %slice.41), channel_id=1, replica_groups=mesh['grp'=16,'rep'=48] {'grp'}, dimensions={2}, use_global_device_ids=true | all-gather | bytes 557056 | tf_op jit(solution)/shard_map/all_gather | solution.py:95
  200.1 0.8 copy-done.2
  200.9 0.2 fusion.12
  201.0 1.5 fusion.9
  202.6 0.2 reshape.416
  202.8 0.4 fusion.4
  203.1 0.1 copy.39
  203.3 0.9 reshape.434
  204.2 4.7 %all-to-all-start.1 = ((bf16[48,2,1024]{2,1,0:T(2,128)(2,1)}), bf16[48,2,1024]{2,1,0:T(2,128)(2,1)S(1)}, u32[]{:S(2)}, u32[]{:S(2)}) async-start(bf16[48,2,1024]{2,1,0:T(2,128)(2,1)} %reshape.434), calls=%async_computation.2 | async-start | bytes 393216 | tf_op jit(solution)/shard_map/all_to_all | solution.py:123
  208.9 0.0 copy-start.4
  208.9 0.0 copy-start.5
  208.9 1.1 convolution_bitcast_fusion.5
  210.0 1.0 convolution_bitcast_fusion.6
  211.0 1.3 convolution_bitcast_fusion.7
  212.3 1.3 convolution_bitcast_fusion.8
  213.6 0.0 copy-done.3
  213.7 0.3 convolution_bitcast_fusion.4
  214.0 0.0 copy-done.7
  214.0 0.8 fusion.32
  214.8 0.8 fusion.33
  215.5 7.9 %all-to-all-done.1 = bf16[48,2,1024]{2,1,0:T(2,128)(2,1)S(1)} async-done(((bf16[48,2,1024]{2,1,0:T(2,128)(2,1)}), bf16[48,2,1024]{2,1,0:T(2,128)(2,1)S(1)}, u32[]{:S(2)}, u32[]{:S(2)}) %all-to-all-start.1) | async-done | bytes 196640 | tf_op jit(solution)/shard_map/all_to_all | solution.py:123
  223.4 0.3 reshape.435
  223.7 0.3 fusion.5
  224.0 0.7 copy.26
  (22 shorter events, 0.1 us)
Async XLA Ops:
  7.2 193.9 %copy-start = (bf16[1,4,512,512]{3,2,1,0:T(8,128)(2,1)S(1)}, bf16[1,4,512,512]{3,2,1,0:T(8,128)(2,1)}, u32[]{:S(2)}) copy-start(bf16[1,4,512,512]{3,2,1,0:T(8,128)(2,1)} %param.12) | copy-start | bytes 6291460
  7.2 83.6 %reduce-scatter.2.cloned.1.call-start = ((), (), s32[]{:S(2)}) async-start(), calls=%async_computation.3 | async-start | bytes 6684672 | tf_op jit(solution)/shard_map/reduce_scatter | solution.py:56
  12.7 0.7 copy-start.12
  12.7 2.0 copy-start.10
  92.2 65.5 %copy-start.9 = (bf16[1,4,512,32]{2,3,1,0:T(8,128)(2,1)S(1)}, bf16[1,4,512,32]{2,3,1,0:T(8,128)(2,1)}, u32[]{:S(2)}) copy-start(bf16[1,4,512,32]{2,3,1,0:T(8,128)(2,1)} %param.13) | copy-start | bytes 393220
  93.2 24.3 %all-to-all-start = ((bf16[48,2,1024]{2,1,0:T(2,128)(2,1)}), bf16[48,2,1024]{2,1,0:T(2,128)(2,1)S(1)}, u32[]{:S(2)}, u32[]{:S(2)}) async-start(bf16[48,2,1024]{2,1,0:T(2,128)(2,1)} %reshape.432), calls=%async_computation.1 | async-start | bytes 393216 | tf_op jit(solution)/shard_map/all_to_all | solution.py:68
  178.5 0.8 copy-start.1
  200.1 0.8 copy-start.2
  204.2 9.8 %copy-start.6 = (f32[1,1,32,512]{3,2,1,0:T(8,128)S(1)}, f32[1,1,32,512]{3,2,1,0:T(8,128)}, u32[]{:S(2)}) copy-start(f32[1,1,32,512]{3,2,1,0:T(8,128)} %convolution_bitcast_fusion.1) | copy-start | bytes 196612
  204.2 9.8 %copy-start.7 = (f32[1,1,32,512]{3,2,1,0:T(8,128)S(1)}, f32[1,1,32,512]{3,2,1,0:T(8,128)}, u32[]{:S(2)}) copy-start(f32[1,1,32,512]{3,2,1,0:T(8,128)} %convolution_bitcast_fusion.2) | copy-start | bytes 196612
  204.2 9.8 %copy-start.8 = (f32[1,1,32,512]{3,2,1,0:T(8,128)S(1)}, f32[1,1,32,512]{3,2,1,0:T(8,128)}, u32[]{:S(2)}) copy-start(f32[1,1,32,512]{3,2,1,0:T(8,128)} %convolution_bitcast_fusion.3) | copy-start | bytes 196612
  204.2 19.2 %all-to-all-start.1 = ((bf16[48,2,1024]{2,1,0:T(2,128)(2,1)}), bf16[48,2,1024]{2,1,0:T(2,128)(2,1)S(1)}, u32[]{:S(2)}, u32[]{:S(2)}) async-start(bf16[48,2,1024]{2,1,0:T(2,128)(2,1)} %reshape.434), calls=%async_computation.2 | async-start | bytes 393216 | tf_op jit(solution)/shard_map/all_to_all | solution.py:123
  208.8 4.8 %copy-start.3 = (bf16[1,512,512]{1,2,0:T(8,128)(2,1)S(1)}, bf16[1,512,512]{1,2,0:T(8,128)(2,1)}, u32[]{:S(2)}) copy-start(bf16[1,512,512]{1,2,0:T(8,128)(2,1)} %copy-done.2) | copy-start | bytes 1572868
  208.9 5.1 %copy-start.4 = (f32[1,4,32,512]{3,2,1,0:T(8,128)S(1)}, f32[1,4,32,512]{3,2,1,0:T(8,128)}, u32[]{:S(2)}) copy-start(f32[1,4,32,512]{3,2,1,0:T(8,128)} %param.10) | copy-start | bytes 786436
  208.9 5.9 %copy-start.5 = (f32[1,4,32,512]{3,2,1,0:T(8,128)S(1)}, f32[1,4,32,512]{3,2,1,0:T(8,128)}, u32[]{:S(2)}) copy-start(f32[1,4,32,512]{3,2,1,0:T(8,128)} %param.11) | copy-start | bytes 786436
  211.0 12.7 %copy-start.11 = (pred[20]{0:T(512)(128)(4,1)S(1)}, pred[20]{0:T(512)(128)(4,1)}, u32[]{:S(2)}) copy-start(pred[20]{0:T(512)(128)(4,1)} %get-tuple-element.21) | copy-start | bytes 64
Sparse Core Ops, SparseCore 0:
  12.8 77.8 reduce-scatter.1
where the time goes:
time: 233 us; the launch traced here: 232 us
  waiting for transfers between devices  95.4 us (41%)
  blocking collectives  72.1 us (31%)
  starting transfers between devices  16.1 us (7%)
  local copies, waits for them, and re-layouts  15.2 us (7%)
  between operations  15 us (6%)
  matrix products  14.2 us (6%)
  other arithmetic  3.45 us (1%)
    reduce_scatter x1, waiting for transfers between devices, on_device(): lax.psum_scatter(grad_part[0], 'grp', scatter_dimension=2, tiled=True)  74.9 us
    all_gather x4, blocking collectives, on_device(): lax.all_gather(single, 'grp', axis=2, tiled=True)  72.1 us
    all_to_all x1, waiting for transfers between devices, on_device(): lax.all_to_all(outgoing, 'rep', split_axis=0, concat_axis=0, tiled=True)  12.6 us
    all_to_all x1, starting transfers between devices, on_device(): lax.all_to_all(outgoing, 'rep', split_axis=0, concat_axis=0, tiled=True)  11.4 us
    unnamed x32, local copies, waits for them, and re-layouts  10 us
    all_to_all x1, waiting for transfers between devices, on_device(): lax.all_to_all(homeward, 'rep', split_axis=0, concat_axis=0, tiled=True)  7.91 us
    dot_general x4, matrix products, absorb(): jnp.einsum('sia,sib->sab', owned_cols, piece, preferred_element_type=jnp....  4.76 us
  transfers between devices with their start and end apart: 3, of which 3 were waited for; matrix products, arithmetic and copies ran while one was open for 4% of the time, Pallas kernels for 0%

commit v1 on v0

v1 whole, which is shorter than its diff:
```python
import jax
import jax.numpy as jnp
from jax import lax
from jax.experimental import pallas as pl
from jax.experimental.pallas import tpu as pltpu
from jax.sharding import PartitionSpec as P

MESH = pl.DeviceIdType.MESH
f32 = jnp.float32
bf16 = jnp.bfloat16

decay = 0.95

NX, NZ, NY = 4, 12, 8
N_REP = NX * NZ
COLS = 20
SLOTS = 4
PARTS = 8
NT = (((1,), (1,)), ((), ()))
NN = (((1,), (0,)), ((), ()))
ZERO_PIECE = COLS
ZERO_TILE = N_REP
ZERO_RESULT = SLOTS * PARTS
TAB_B, TAB_C = 0, N_REP
TAB_D = TAB_C + SLOTS * PARTS
TAB_E = TAB_D + N_REP
ORDER = (4, 3, 5, 2, 6, 1, 7, 0)
HALF = COLS // 2


def kernel(
    tab, x_hbm, lstat_hbm, rstat_hbm, lroot_hbm, rroot_hbm,
    upd_ref, lout_ref, rout_ref,
    own, sib, send_a, recv_a, tiles, send_b, recv_b, gath, res, send_d, recv_d, spread,
    lstat, rstat, lroot, rroot,
    own_sem, load_sem, sib_ssem, sib_rsem, a_ssem, a_rsem, b_sem, c_ssem, c_rsem, k_ssem, k_rsem, d_sem,
):
    g = lax.axis_index("grp")
    p = lax.axis_index("rep")
    y = lax.div(g, 2)
    core = lax.rem(g, 2)
    px = lax.div(p, NZ)
    pz = lax.rem(p, NZ)
    sibling = g + 1 - 2 * core
    up = lax.rem(y + 1, NY) * 2 + core
    down = lax.rem(y + NY - 1, NY) * 2 + core

    def peer(n):
        dx = lax.div(n, NZ)
        dz = lax.rem(n, NZ)
        return lax.rem(px + dx, NX) * NZ + lax.rem(pz + dz, NZ)

    def remote(src, dst, ssem, rsem, grp, rep):
        return pltpu.make_async_remote_copy(
            src_ref=src, dst_ref=dst, send_sem=ssem, recv_sem=rsem, device_id=(grp, rep), device_id_type=MESH
        )

    def piece_of(k, who_core):
        there = lax.rem(y + k, NY)
        row = pl.multiple_of(lax.div(there, 2) * 16, 16)
        col = pl.multiple_of((lax.rem(there, 2) * 2 + who_core) * 128, 128)
        return x_hbm.at[0, pl.ds(row, 16), :, pl.ds(col, 128)]

    own_loads = {k: pltpu.make_async_copy(piece_of(k, core), own.at[k], own_sem.at[k]) for k in ORDER}
    for k in ORDER:
        own_loads[k].start()
    late_loads = [
        pltpu.make_async_copy(src, dst, load_sem.at[i])
        for i, (src, dst) in enumerate(
            ((lstat_hbm.at[0], lstat), (rstat_hbm.at[0], rstat), (lroot_hbm.at[0], lroot), (rroot_hbm, rroot))
        )
    ]
    for one in late_loads:
        one.start()

    barrier = pltpu.get_barrier_semaphore()
    for who in (sibling, up, down):
        pl.semaphore_signal(barrier, inc=1, device_id=(who, p), device_id_type=MESH)

    def greet(n, carry):
        pl.semaphore_signal(barrier, inc=1, device_id=(g, peer(n)), device_id_type=MESH)
        return carry

    lax.fori_loop(1, N_REP, greet, 0)
    tiles[ZERO_PIECE] = jnp.zeros((16, 128), bf16)
    recv_b[ZERO_TILE] = jnp.zeros((16, 128), bf16)
    res[ZERO_RESULT] = jnp.zeros((16, 128), bf16)
    pl.semaphore_wait(barrier, N_REP - 1 + 3)

    pair = {
        k: remote(piece_of(k, 1 - core), sib.at[k], sib_ssem.at[k], sib_rsem.at[k], sibling, p) for k in ORDER
    }
    for k in ORDER:
        pair[k].start()

    def pair_sum(k, j):
        return own[k, :, j, :] + sib[k, :, j, :]

    arrived = set()

    def need(k):
        if k not in arrived:
            arrived.add(k)
            own_loads[k].wait()
            pair[k].wait_recv()

    def chain(way, dist, part):
        slot = (way * 4 + dist - 1) * 2 + part
        span = pl.ds(part * HALF, HALF)
        return remote(
            send_a.at[way, dist - 1, span], recv_a.at[way, dist - 1, span],
            a_ssem.at[slot], a_rsem.at[slot], down if way else up, p,
        )

    def send_sum(way, dist, part, from_dist):
        k = NY - dist if way else dist
        need(k)
        if from_dist:
            chain(way, from_dist, part).wait_recv()
        for j in range(part * HALF, part * HALF + HALF):
            total = pair_sum(k, j)
            if from_dist:
                total = total + recv_a[way, from_dist - 1, j].astype(f32)
            send_a[way, dist - 1, j] = total.astype(bf16)
        chain(way, dist, part).start()

    for way in range(2):
        send_sum(way, 4, way, None)
    for way in range(2):
        send_sum(way, 3, 1 - way, None)
    for way in range(2):
        send_sum(way, 3, way, 4)
    for dist in (2, 1):
        for part in range(2):
            for way in range(2):
                send_sum(way, dist, (1 - part) if way == 0 else part, dist + 1)
    need(0)
    for part in range(2):
        for way in range(2):
            chain(way, 1, part).wait_recv()
        for j in range(part * HALF, part * HALF + HALF):
            total = pair_sum(0, j) + recv_a[0, 0, j].astype(f32) + recv_a[1, 0, j].astype(f32)
            tiles[j] = total.astype(bf16)

    recv_b[0] = tiles[tab[TAB_B]]

    def send_piece(n, carry):
        send_b[n] = tiles[tab[TAB_B + n]]
        remote(send_b.at[n], recv_b.at[n], b_sem.at[0], b_sem.at[1], g, peer(n)).start()
        return carry

    lax.fori_loop(1, N_REP, send_piece, 0)
    rest = pl.ds(1, N_REP - 1)
    all_b = remote(send_b.at[rest], recv_b.at[rest], b_sem.at[0], b_sem.at[1], g, p)
    all_b.wait_recv()

    def home(y_of, core_of, s):
        who = y_of * 2 + core_of
        return gath.at[s, lax.rem(who, 4), :, lax.div(who, 4)]

    for s in range(SLOTS):
        for u in range(PARTS):
            gath[s, lax.rem(g, 4), u, lax.div(g, 4)] = recv_b[tab[TAB_C + s * PARTS + u]]

    def ring(way, dist, s, y_of):
        place = home(y_of, core, s)
        index = (way * 4 + dist - 1) * SLOTS + s
        return remote(place, place, c_ssem.at[index], c_rsem.at[index], down if way else up, p)

    def across(index, s, y_of, core_of):
        place = home(y_of, core_of, s)
        return remote(place, place, k_ssem.at[index * SLOTS + s], k_rsem.at[index * SLOTS + s], sibling, p)

    def back(way, dist):
        return lax.rem(y + dist, NY) if way else lax.rem(y + NY - dist, NY)

    def carries(way, dist, s):
        return dist < 4 or (s >= SLOTS // 2) == bool(way)

    def relay(way, dist):
        return way * 4 + dist

    for s in range(SLOTS):
        for way in range(2):
            ring(way, 1, s, y).start()
        across(0, s, y, core).start()
    for dist in range(1, 5):
        for s in range(SLOTS):
            for way in range(2):
                if not carries(way, dist, s):
                    continue
                origin = back(way, dist)
                ring(way, dist, s, origin).wait_recv()
                if dist < 4 and carries(way, dist + 1, s):
                    ring(way, dist + 1, s, origin).start()
                across(relay(way, dist), s, origin, core).start()

    for one in late_loads:
        one.wait()
    lanes = lax.broadcasted_iota(jnp.int32, (32, 512), 1)
    picks = lax.broadcasted_iota(jnp.int32, (32, 512), 0) + g * 32
    pick = jnp.where(lanes == picks, 1.0, 0.0).astype(bf16)
    lane_group = lax.div(lax.broadcasted_iota(jnp.int32, (512, 128), 1), 32)

    for s in range(SLOTS):
        across(0, s, y, 1 - core).wait_recv()
        for way in range(2):
            for dist in range(1, 5):
                if carries(way, dist, s):
                    across(relay(way, dist), s, back(way, dist), 1 - core).wait_recv()

    def products(s, carry):
        whole = jnp.concatenate([gath[s, q].reshape(512, 128) for q in range(4)], axis=1)
        band = pl.ds(lax.rem(g, 2) * 2, 2)
        mine = jnp.concatenate(
            [gath[s, q, lax.div(g, 2), band].reshape(32, 128) for q in range(4)], axis=1
        )
        first = lax.dot_general(jnp.concatenate([mine, pick], axis=0), whole, NT, preferred_element_type=f32)
        lout_ref[0, s] = decay * lstat[s] + (1.0 - decay) * first[:32]
        strip = first[32:].astype(bf16)
        second = lax.dot_general(strip, whole, NN, preferred_element_type=f32)
        rout_ref[0, s] = decay * rstat[s] + (1.0 - decay) * second
        mixed = lax.dot_general(whole, rroot[s], NN, preferred_element_type=f32)
        packed = jnp.zeros((128, 128), f32)
        for q in range(4):
            quarter = jnp.where(lane_group == q, mixed, 0.0).astype(bf16)
            factor = lroot[s, :, q].reshape(128, 512)
            packed = packed + lax.dot_general(factor, quarter, NN, preferred_element_type=f32)
        res[pl.ds(s * PARTS, PARTS)] = packed.astype(bf16).reshape(PARTS, 16, 128)
        return carry

    lax.fori_loop(0, SLOTS, products, 0)

    recv_d[0] = res[tab[TAB_D]]

    def send_rows(n, carry):
        send_d[n] = res[tab[TAB_D + n]]
        remote(send_d.at[n], recv_d.at[n], d_sem.at[0], d_sem.at[1], g, peer(n)).start()
        return carry

    lax.fori_loop(1, N_REP, send_rows, 0)
    all_d = remote(send_d.at[rest], recv_d.at[rest], d_sem.at[0], d_sem.at[1], g, p)
    all_d.wait_recv()

    def unpack(j, carry):
        rows = recv_d[tab[TAB_E + j]].astype(f32)
        for q in range(4):
            spread[j, pl.ds(q * 16, 16), :] = pltpu.roll(rows, (128 - 32 * q) % 128, 1)
        return carry

    lax.fori_loop(0, COLS, unpack, 0)
    for j in range(COLS):
        upd_ref[:, j, :] = spread[j, :, 0:32].astype(bf16)

    for k in ORDER:
        pair[k].wait_send()
    for way in range(2):
        for dist in range(1, 5):
            for part in range(2):
                if dist < 4 or part == way:
                    chain(way, dist, part).wait_send()
    all_b.wait_send()
    for s in range(SLOTS):
        across(0, s, y, core).wait_send()
        for way in range(2):
            for dist in range(1, 5):
                if carries(way, dist, s):
                    ring(way, dist, s, y).wait_send()
                    across(relay(way, dist), s, y, core).wait_send()
    all_d.wait_send()


def tables(owners, readers):
    me = lax.axis_index("rep").astype(jnp.int32)
    mx, mz = me // NZ, me % NZ
    n = jnp.arange(N_REP, dtype=jnp.int32)
    dest = (mx + n // NZ) % NX * NZ + (mz + n % NZ) % NZ

    def rel(src):
        return (mx - src // NZ) % NX * NZ + (mz - src % NZ) % NZ

    cols = jnp.arange(COLS, dtype=jnp.int32)
    targets = lax.dynamic_index_in_dim(owners, me // PARTS, 0, keepdims=False)
    tab_b = jnp.min(jnp.where(targets[None, :] == dest[:, None], cols[None, :], ZERO_PIECE), axis=1)
    has = jnp.any(owners == me, axis=1)
    rows = jnp.arange(owners.shape[0], dtype=jnp.int32)
    slot = jnp.sum((has[None, :] & (rows[None, :] < rows[:, None])).astype(jnp.int32), axis=1)
    slots = jnp.arange(SLOTS, dtype=jnp.int32)
    hit = has[None, :] & (slot[None, :] == slots[:, None])
    row_of = jnp.sum(jnp.where(hit, rows[None, :], 0), axis=1)
    filled = jnp.any(hit, axis=1)
    parts = jnp.arange(PARTS, dtype=jnp.int32)
    tab_c = jnp.where(filled[:, None], rel(row_of[:, None] * PARTS + parts[None, :]), ZERO_TILE)
    source = jnp.sum(jnp.where(readers[None, :] == dest[:, None], n[None, :], 0), axis=1)
    in_row = (source // PARTS)[:, None] == rows[None, :]
    place = jnp.sum(jnp.where(in_row & has[None, :], slot[None, :] + 1, 0), axis=1)
    tab_d = jnp.where(place > 0, (place - 1) * PARTS + source % PARTS, ZERO_RESULT)
    my_source = jnp.sum(jnp.where(readers == me, n, 0))
    row_owners = lax.dynamic_index_in_dim(owners, my_source // PARTS, 0, keepdims=False)
    tab_e = rel(row_owners)
    return jnp.concatenate([tab_b, tab_c.reshape(-1), tab_d, tab_e])


def on_device(grad_part, owners, readers, left_stat, right_stat, left_root, right_root):
    tab = tables(owners, readers)
    roots = left_root.reshape(1, SLOTS, PARTS, 4, 16, 512)
    strips = jnp.tile(right_root[0], (1, 1, 4))
    hbm = pl.BlockSpec(memory_space=pl.ANY)
    vmem = pl.BlockSpec(memory_space=pltpu.VMEM)
    dma = pltpu.SemaphoreType.DMA
    return pl.pallas_call(
        kernel,
        out_shape=(
            jax.ShapeDtypeStruct((64, COLS, 32), bf16),
            jax.ShapeDtypeStruct(left_stat.shape, f32),
            jax.ShapeDtypeStruct(right_stat.shape, f32),
        ),
        in_specs=[pl.BlockSpec(memory_space=pltpu.SMEM)] + [hbm] * 5,
        out_specs=(vmem, vmem, vmem),
        scratch_shapes=[
            pltpu.VMEM((NY, 16, COLS, 128), f32),
            pltpu.VMEM((NY, 16, COLS, 128), f32),
            pltpu.VMEM((2, 4, COLS, 16, 128), bf16),
            pltpu.VMEM((2, 4, COLS, 16, 128), bf16),
            pltpu.VMEM((COLS + 1, 16, 128), bf16),
            pltpu.VMEM((N_REP, 16, 128), bf16),
            pltpu.VMEM((N_REP + 1, 16, 128), bf16),
            pltpu.VMEM((SLOTS, 4, PARTS, 4, 16, 128), bf16),
            pltpu.VMEM((SLOTS * PARTS + 1, 16, 128), bf16),
            pltpu.VMEM((N_REP, 16, 128), bf16),
            pltpu.VMEM((N_REP, 16, 128), bf16),
            pltpu.VMEM((COLS, 64, 128), f32),
            pltpu.VMEM((SLOTS, 32, 512), f32),
            pltpu.VMEM((SLOTS, 32, 512), f32),
            pltpu.VMEM((SLOTS, PARTS, 4, 16, 512), bf16),
            pltpu.VMEM((SLOTS, 512, 128), bf16),
            dma((NY,)), dma((4,)), dma((NY,)), dma((NY,)), dma((16,)), dma((16,)), dma((2,)),
            dma((8 * SLOTS,)), dma((8 * SLOTS,)), dma((9 * SLOTS,)), dma((9 * SLOTS,)), dma((2,)),
        ],
        compiler_params=pltpu.CompilerParams(
            collective_id=0, has_side_effects=True, vmem_limit_bytes=48 * 1024 * 1024
        ),
        cost_estimate=pl.CostEstimate(flops=300_000_000, bytes_accessed=8_000_000, transcendentals=0),
    )(tab, grad_part, left_stat, right_stat, roots, strips)


def solution(mesh):
    placed = (
        P("grp", "rep", None, None),
        P(),
        P(),
        P("rep", None, "grp", None),
        P("rep", None, "grp", None),
        P("rep", None, None, None),
        P("rep", None, None, "grp"),
    )
    return jax.shard_map(
        on_device,
        mesh=mesh,
        in_specs=placed,
        out_specs=(P("rep", None, "grp"), P("rep", None, "grp", None), P("rep", None, "grp", None)),
        check_vma=False,
    )
```

time: 233 us -> 102 us (0.44)
  waiting for transfers between devices: 95.4 us -> 0 us
  Pallas kernels: 0 us -> 83.7 us
  blocking collectives: 72.1 us -> 0 us
  starting transfers between devices: 16.1 us -> 0 us
  matrix products: 14.2 us -> 0 us
  between operations: 15 us -> 3.38 us
  local copies, waits for them, and re-layouts: 15.2 us -> 9.79 us
    pallas_call x0 -> x1, Pallas kernels: none -> 83.7 us  [on_device(): pl.pallas_call(kernel, out_shape=(jax.ShapeDtypeStruct((64, COLS, 32), bf...]
    reduce_scatter x1 -> x0, waiting for transfers between devices: 74.9 us -> none  [on_device(): lax.psum_scatter(grad_part[0], 'grp', scatter_dimension=2, tiled=True)]
    all_gather x4 -> x0, blocking collectives: 72.1 us -> none  [on_device(): lax.all_gather(single, 'grp', axis=2, tiled=True)]
    all_to_all x2 -> x0, waiting for transfers between devices: 20.5 us -> none  [the longest x1 12.6 us: on_device(): lax.all_to_all(outgoing, 'rep', split_axis=0, concat_axis=0, tiled=True)]
    all_to_all x2 -> x0, starting transfers between devices: 16.1 us -> none  [the longest x1 11.4 us: on_device(): lax.all_to_all(outgoing, 'rep', split_axis=0, concat_axis=0, tiled=True)]
    dot_general x17 -> x0, matrix products: 14.2 us -> none  [the longest x4 4.76 us: absorb(): jnp.einsum('sia,sib->sab', owned_cols, piece, preferred_element_type=jnp....]
    unnamed x32 -> x9, local copies, waits for them, and re-layouts: 10 us -> 6.53 us
  transfers between devices with their start and end apart: 3 -> 0, of which waited for: 3 -> 0; matrix products, arithmetic and copies ran while one was open for 4% -> 0% of each run, Pallas kernels for 0% -> 0%
where the time goes in v1:
time: 102 us; the launch traced here: 101 us
  Pallas kernels  83.7 us (82%)
  local copies, waits for them, and re-layouts  9.79 us (10%)
  other arithmetic  4.49 us (4%)
  between operations  3.38 us (3%)
    pallas_call x1, Pallas kernels, on_device(): pl.pallas_call(kernel, out_shape=(jax.ShapeDtypeStruct((64, COLS, 32), bf...  83.7 us
    unnamed x9, local copies, waits for them, and re-layouts  6.53 us

profile of v1, /device:TPU:1, one launch (start us, length us, event | category | flops | bytes accessed | tf_op | source)
XLA Modules:
  0.0 101.4 jit_solution(8244409516715024458)
XLA Ops:
  0.7 0.7 dynamic-slice_bitcast_fusion
  1.4 0.8 compare_reduce_fusion
  2.2 0.1 convert_reduce_fusion
  2.3 0.1 select_reduce_fusion.1
  2.4 0.8 select_reduce_fusion
  3.3 0.1 select_reduce_fusion.3
  3.4 0.1 sign_compare_fusion
  3.5 0.1 ne.189
  3.6 0.1 select_reduce_fusion.2
  3.7 0.1 fusion.6
  3.8 1.3 %compare_select_fusion.7 = (s32[48]{0:T(128)S(1)}, s32[]{:T(128)}) fusion(s32[48]{0:T(128)S(1)} %select_reduce_fusion.2, s32[48]{0:T(128)S(1)} %select_reduce_fusion, s32[48]{0:T(128)} %param.9, s32[]{:T(128)S(6)} %axis_index.12), kind=kLoop, calls=%fused_computation.29 | loop fusion | flops 911 | bytes 776 | tf_op jit(solution)/shard_map/jit(_where)/select_n | solution.py:297
  7.7 0.7 fusion.12
  8.4 0.1 broadcast_in_dim.89
  8.5 0.1 broadcast_in_dim.90
  8.6 0.1 fusion.2
  8.7 0.1 div.61
  8.7 0.1 rem.200
  8.9 0.1 pad_add_fusion.tab
  8.9 0.9 tile.11
  9.9 0.3 copy.17.rroot_hbm
  10.2 0.0 copy-start
  10.2 0.0 copy-start.1
  10.2 0.0 copy-start.2
  10.2 5.1 %copy.16.x_hbm = f32[1,64,20,512]{3,2,1,0:T(8,128)} copy(f32[1,64,20,512]{3,1,2,0:T(8,128)} %param.7) | data formatting | bytes 5242880 | tf_op args[0]
  15.3 0.0 copy-done
  15.3 0.0 copy-done.1
  15.3 0.0 copy-done.2
  15.3 83.7 %shard_map.94 = (bf16[64,20,32]{2,1,0:T(8,128)(2,1)S(1)}, f32[1,4,32,512]{3,2,1,0:T(8,128)S(1)}, f32[1,4,32,512]{3,2,1,0:T(8,128)S(1)}) custom-call(s32[148]{0:T(256)S(1)} %pad_add_fusion.tab, f32[1,64,20,512]{3,2,1,0:T(8,128)} %copy.16.x_hbm, f32[1,4,32,512]{3,2,1,0:T(8,128)S(1)} %copy-done.1, f32[1,4,32,512]{3,2,1,0:T(8,128)S(1)} %copy-done.2, ...), custom_call_target="tpu_custom_call" | custom-call | flops 300000000 | bytes 8000000 | tf_op jit(solution)/shard_map/pallas_call | solution.py:311
  99.1 0.9 copy.18
  100.0 0.7 copy.21
  100.7 0.7 copy.22
  (5 shorter events, 0.1 us)
Async XLA Ops:
  10.2 5.1 %copy-start = (bf16[1,4,512,512]{3,2,1,0:T(8,128)(2,1)S(1)}, bf16[1,4,512,512]{3,2,1,0:T(8,128)(2,1)}, u32[]{:S(2)}) copy-start(bf16[1,4,512,512]{3,2,1,0:T(8,128)(2,1)} %param.12) | copy-start | bytes 6291460
  10.2 5.1 %copy-start.1 = (f32[1,4,32,512]{3,2,1,0:T(8,128)S(1)}, f32[1,4,32,512]{3,2,1,0:T(8,128)}, u32[]{:S(2)}) copy-start(f32[1,4,32,512]{3,2,1,0:T(8,128)} %lstat_hbm.1) | copy-start | bytes 786436
  10.2 5.1 %copy-start.2 = (f32[1,4,32,512]{3,2,1,0:T(8,128)S(1)}, f32[1,4,32,512]{3,2,1,0:T(8,128)}, u32[]{:S(2)}) copy-start(f32[1,4,32,512]{3,2,1,0:T(8,128)} %rstat_hbm.1) | copy-start | bytes 786436

commit v2 on v1

v2 whole, which is shorter than its diff:
```python
import jax
import jax.numpy as jnp
from jax import lax
from jax.experimental import pallas as pl
from jax.experimental.pallas import tpu as pltpu
from jax.sharding import PartitionSpec as P

MESH = pl.DeviceIdType.MESH
f32 = jnp.float32
bf16 = jnp.bfloat16

decay = 0.95

NX, NZ, NY = 4, 12, 8
N_REP = NX * NZ
BLOCK_ROWS = 6
COLS = 20
SLOTS = 4
PARTS = 8
NT = (((1,), (1,)), ((), ()))
NN = (((1,), (0,)), ((), ()))
ZERO_PIECE = COLS
ZERO_TILE = N_REP
ZERO_RESULT = SLOTS * PARTS
TAB_B, TAB_C, TAB_D, TAB_E = 0, 1, 2, 3
PLANE = [(dx, dz) for i in (5, 4, 3, 2, 1, 0) for dz in (i, NZ - 1 - i) for dx in range(NX) if dx or dz]
HALF = COLS // 2
QUARTER = COLS // 4


def kernel(
    owners, readers, x_hbm, lstat_hbm, rstat_hbm, lroot_hbm, rroot_hbm,
    upd_hbm, lout_hbm, rout_hbm,
    own, sib, send_a, recv_a, tiles, send_b, recv_b, gath, res, send_d, recv_d,
    lstat, rstat, lroot, rroot, lout, rout, upd, tab_v, tab,
    own_sem, load_sem, tab_sem, sib_ssem, sib_rsem, a_ssem, a_rsem, b_sem, c_ssem, c_rsem, k_ssem, k_rsem, d_sem,
    round_sem, out_sem,
):
    g = lax.axis_index("grp")
    p = lax.axis_index("rep")
    y = lax.div(g, 2)
    core = lax.rem(g, 2)
    px = lax.div(p, NZ)
    pz = lax.rem(p, NZ)
    sibling = g + 1 - 2 * core
    up = lax.rem(y + 1, NY) * 2 + core
    down = lax.rem(y + NY - 1, NY) * 2 + core
    at_x = [lax.rem(px + dx, NX) * NZ for dx in range(NX)]
    at_z = [lax.rem(pz + dz, NZ) for dz in range(NZ)]

    def peer(dx, dz):
        return at_x[dx % NX] + at_z[dz % NZ]

    def remote(src, dst, ssem, rsem, grp, rep):
        return pltpu.make_async_remote_copy(
            src_ref=src, dst_ref=dst, send_sem=ssem, recv_sem=rsem, device_id=(grp, rep), device_id_type=MESH
        )

    def rows_of(half, who_core, part):
        row = pl.multiple_of(who_core * 32 + half * 16, 16)
        return x_hbm.at[pl.ds(part * HALF, HALF), pl.ds(row, 16)]

    batches = [(i, half, part) for i, (half, part) in enumerate(((0, 0), (0, 1), (1, 0), (1, 1)))]

    def strip_of(k):
        there = lax.rem(y + k, NY)
        half = lax.div(there, 4)
        cols = pl.ds(pl.multiple_of(lax.rem(there, 4) * 128, 128), 128)
        rows = pl.ds(pl.multiple_of((1 - core) * 32 + half * 16, 16), 16)
        return remote(
            x_hbm.at[:, rows, cols], sib.at[k], sib_ssem.at[k], sib_rsem.at[k], sibling, p
        )

    def band(ref, half, part):
        return ref.at[half, pl.ds(part * HALF, HALF)]

    own_loads = [
        pltpu.make_async_copy(rows_of(half, core, part), band(own, half, part), own_sem.at[i])
        for i, half, part in batches
    ]
    for one in own_loads:
        one.start()

    barrier = pltpu.get_barrier_semaphore()
    for who in (sibling, up, down):
        pl.semaphore_signal(barrier, inc=1, device_id=(who, p), device_id_type=MESH)

    for dx, dz in ((1, 0), (-1, 0), (0, 1), (0, -1)):
        pl.semaphore_signal(barrier, inc=1, device_id=(g, peer(dx, dz)), device_id_type=MESH)
    tiles[ZERO_PIECE] = jnp.zeros((16, 128), bf16)
    recv_b[ZERO_TILE] = jnp.zeros((16, 128), bf16)
    res[ZERO_RESULT] = jnp.zeros((16, 128), bf16)
    pl.semaphore_wait(barrier, 7)

    rounds = (
        ((0, 1), (0, -1)), ((0, 2), (0, -2)), ((0, 2), (0, -2)), ((1, 0), (-1, 0)), ((1, 0),),
    )

    def tell(i):
        for dx, dz in rounds[i]:
            pl.semaphore_signal(round_sem.at[i], inc=1, device_id=(g, peer(dx, dz)), device_id_type=MESH)

    def hear(i):
        pl.semaphore_wait(round_sem.at[i], len(rounds[i]))
        if i + 1 < len(rounds):
            tell(i + 1)

    strip_of(4).start()
    tell(0)
    late_loads = [
        pltpu.make_async_copy(src, dst, load_sem.at[i])
        for i, (src, dst) in enumerate(
            ((lstat_hbm.at[0], lstat), (rstat_hbm.at[0], rstat), (lroot_hbm.at[0], lroot), (rroot_hbm, rroot))
        )
    ]
    for one in late_loads:
        one.start()
    fill_tables(owners, readers, tab_v, p, px, pz)
    tab_copy = pltpu.make_async_copy(tab_v, tab, tab_sem.at[0])
    tab_copy.start()
    strip_of(3).start()
    strip_of(5).start()
    hear(0)
    for one in own_loads:
        one.wait()

    def pair_sum(k, j):
        there = lax.rem(y + k, NY)
        at = (lax.div(there, 4), j, slice(None), pl.ds(pl.multiple_of(lax.rem(there, 4) * 128, 128), 128))
        return own[at] + sib[k, j]

    arrived = set()

    def need(k):
        if k not in arrived:
            arrived.add(k)
            strip_of(k).wait_recv()

    def chain(way, dist, part):
        slot = (way * 4 + dist - 1) * 4 + part
        span = pl.ds(part * QUARTER, QUARTER)
        return remote(
            send_a.at[way, dist - 1, span], recv_a.at[way, dist - 1, span],
            a_ssem.at[slot], a_rsem.at[slot], down if way else up, p,
        )

    def span_of(part):
        return range(part * QUARTER, part * QUARTER + QUARTER)

    def send_sum(way, dist, part, from_dist):
        k = NY - dist if way else dist
        need(k)
        if from_dist:
            chain(way, from_dist, part).wait_recv()
        for j in span_of(part):
            total = pair_sum(k, j)
            if from_dist:
                total = total + recv_a[way, from_dist - 1, j].astype(f32)
            send_a[way, dist - 1, j] = total.astype(bf16)
        chain(way, dist, part).start()

    far_parts = ((0, 1), (2, 3))
    for i in range(2):
        for way in range(2):
            send_sum(way, 4, far_parts[way][i], None)
    strip_of(2).start()
    strip_of(6).start()
    hear(1)
    for i in range(2):
        for way in range(2):
            send_sum(way, 3, far_parts[1 - way][i], None)
    for k in (1, 7, 0):
        strip_of(k).start()
    hear(2)
    for i in range(2):
        for way in range(2):
            send_sum(way, 3, far_parts[way][i], 4)
    for dist in (2, 1):
        hear(5 - dist)
        for i in range(4):
            for way in range(2):
                send_sum(way, dist, (2, 3, 0, 1)[i] if way == 0 else i, dist + 1)
    need(0)
    for part in range(4):
        for way in range(2):
            chain(way, 1, part).wait_recv()
        for j in span_of(part):
            total = pair_sum(0, j) + recv_a[0, 0, j].astype(f32) + recv_a[1, 0, j].astype(f32)
            tiles[j] = total.astype(bf16)

    tab_copy.wait()
    recv_b[0] = tiles[tab[TAB_B, 0]]
    for dx, dz in PLANE:
        n = dx * NZ + dz
        send_b[n] = tiles[tab[TAB_B, n]]
        remote(send_b.at[n], recv_b.at[n], b_sem.at[0], b_sem.at[1], g, peer(dx, dz)).start()
    rest = pl.ds(1, N_REP - 1)
    all_b = remote(send_b.at[rest], recv_b.at[rest], b_sem.at[0], b_sem.at[1], g, p)
    all_b.wait_recv()

    def home(y_of, core_of, s):
        return gath.at[s, lax.rem(y_of, 4), 2 * core_of + lax.div(y_of, 4)]

    for s in range(SLOTS):
        for u in range(PARTS):
            gath[s, lax.rem(y, 4), 2 * core + lax.div(y, 4), u] = recv_b[tab[TAB_C, s * PARTS + u]]

    def ring(way, dist, s, y_of):
        place = home(y_of, core, s)
        index = (way * 4 + dist - 1) * SLOTS + s
        return remote(place, place, c_ssem.at[index], c_rsem.at[index], down if way else up, p)

    def across(index, s, y_of, core_of):
        place = home(y_of, core_of, s)
        return remote(place, place, k_ssem.at[index * SLOTS + s], k_rsem.at[index * SLOTS + s], sibling, p)

    def back(way, dist):
        return lax.rem(y + dist, NY) if way else lax.rem(y + NY - dist, NY)

    def carries(way, dist, s):
        return dist < 4 or s % 2 == way

    def relay(way, dist):
        return way * 4 + dist

    def launch(s):
        for way in range(2):
            ring(way, 1, s, y).start()
        across(0, s, y, core).start()

    def forward(dist, s):
        for way in range(2):
            if carries(way, dist, s):
                origin = back(way, dist)
                ring(way, dist, s, origin).wait_recv()
                if dist < 4 and carries(way, dist + 1, s):
                    ring(way, dist + 1, s, origin).start()
                across(relay(way, dist), s, origin, core).start()

    def gathered(s):
        across(0, s, y, 1 - core).wait_recv()
        for way in range(2):
            for dist in range(1, 5):
                if carries(way, dist, s):
                    across(relay(way, dist), s, back(way, dist), 1 - core).wait_recv()

    left_half = lax.broadcasted_iota(jnp.int32, (16, 128), 1) < 64

    def block_of(s):
        return jnp.concatenate(
            [jnp.concatenate([gath[s, q, h, u] for u in range(PARTS) for h in range(4)], axis=0) for q in range(4)],
            axis=1,
        )

    def precondition(s):
        mixed = lax.dot_general(rroot[s], block_of(s), NT, preferred_element_type=f32).astype(bf16)
        result = lax.dot_general(mixed, lroot[s], NT, preferred_element_type=f32)
        for v in range(PARTS // 2):
            top = result[:16, v * 128 : v * 128 + 128]
            low = result[16:, v * 128 : v * 128 + 128]
            res[s * PARTS + 2 * v] = jnp.where(left_half, top, pltpu.roll(low, 64, 1)).astype(bf16)
            res[s * PARTS + 2 * v + 1] = jnp.where(left_half, pltpu.roll(top, 64, 1), low).astype(bf16)

    groups = ((0, 1), (2, 3))
    for s in groups[0]:
        launch(s)
    for one in late_loads:
        one.wait()
    for s in groups[0]:
        for way in range(2):
            ring(way, 1, s, y).wait_send()
    for s in groups[1]:
        launch(s)
    for dist in range(1, 5):
        for s in range(SLOTS):
            forward(dist, s)
    for s in range(SLOTS):
        gathered(s)
        precondition(s)

    recv_d[0] = res[tab[TAB_D, 0]]
    for dx, dz in PLANE:
        n = dx * NZ + dz
        send_d[n] = res[tab[TAB_D, n]]
        remote(send_d.at[n], recv_d.at[n], d_sem.at[0], d_sem.at[1], g, peer(dx, dz)).start()
    all_d = remote(send_d.at[rest], recv_d.at[rest], d_sem.at[0], d_sem.at[1], g, p)
    lanes = lax.broadcasted_iota(jnp.int32, (32, 512), 1)
    picks = lax.broadcasted_iota(jnp.int32, (32, 512), 0) + g * 32
    pick = jnp.where(lanes == picks, 1.0, 0.0).astype(bf16)
    pair_rows = pl.ds(core * 2, 2)

    def out_copy(src, dst, i):
        return pltpu.make_async_copy(src, dst, out_sem.at[i])

    def out_left(s):
        return out_copy(lout.at[s], lout_hbm.at[0, s], 2 * s)

    def out_right(s):
        return out_copy(rout.at[s], rout_hbm.at[0, s], 2 * s + 1)

    for s in range(SLOTS):
        whole = block_of(s)
        mine = jnp.concatenate([gath[s, q, pair_rows, y].reshape(32, 128) for q in range(4)], axis=1)
        rows = jnp.concatenate([mine, pick], axis=0)
        first = lax.dot_general(rows, whole, NT, preferred_element_type=f32)
        lout[s] = decay * lstat[s] + (1.0 - decay) * first[:32]
        out_left(s).start()
        second = lax.dot_general(first[32:].astype(bf16), whole, NN, preferred_element_type=f32)
        rout[s] = decay * rstat[s] + (1.0 - decay) * second
        out_right(s).start()

    all_d.wait_recv()

    def unpack(j, carry):
        rows = recv_d[tab[TAB_E, j]]
        upd[j, 0:16] = rows[:, 0:64]
        upd[j, 16:32] = pltpu.roll(rows.astype(f32), 64, 1)[:, 0:64].astype(bf16)
        return carry

    lax.fori_loop(0, COLS, unpack, 0, unroll=4)
    out_update = out_copy(upd, upd_hbm, 2 * SLOTS)
    out_update.start()

    for k in range(NY):
        strip_of(k).wait_send()
    for way in range(2):
        for dist in range(1, 5):
            for part in range(4):
                if dist < 4 or part in far_parts[way]:
                    chain(way, dist, part).wait_send()
    all_b.wait_send()
    for s in range(SLOTS):
        across(0, s, y, core).wait_send()
        for way in range(2):
            for dist in range(1, 5):
                if carries(way, dist, s):
                    if dist > 1 or s in groups[1]:
                        ring(way, dist, s, y).wait_send()
                    across(relay(way, dist), s, y, core).wait_send()
    all_d.wait_send()
    for s in range(SLOTS):
        out_left(s).wait()
        out_right(s).wait()
    out_update.wait()


def fill_tables(owners, readers, tab_v, p, px, pz):
    lane = lax.broadcasted_iota(jnp.int32, (1, 128), 1)
    one = jnp.int32(1)
    nil = jnp.int32(0)

    def dozens(v):
        return jnp.where(v >= NZ, one, nil) + jnp.where(v >= 2 * NZ, one, nil) + jnp.where(v >= 3 * NZ, one, nil)

    def rel(src):
        sx = dozens(src)
        dx = px - sx
        dz = pz - (src - NZ * sx)
        return jnp.where(dx < 0, dx + NX, dx) * NZ + jnp.where(dz < 0, dz + NZ, dz)

    hop_x = dozens(lane)
    to_x = px + hop_x
    to_z = pz + lane - NZ * hop_x
    dest = jnp.where(to_x >= NX, to_x - NX, to_x) * NZ + jnp.where(to_z >= NZ, to_z - NZ, to_z)
    my_row = lax.div(p, PARTS)
    piece = jnp.full((1, 128), ZERO_PIECE, jnp.int32)
    for j in range(COLS):
        piece = jnp.where(dest == owners[my_row, j], j, piece)
    tab_v[TAB_B : TAB_B + 1] = piece

    def count(j, held):
        return tuple(jnp.where(owners[i, j] == p, one, h) for i, h in enumerate(held))

    has = lax.fori_loop(0, COLS, count, (nil,) * BLOCK_ROWS)
    slot, total = [], nil
    for i in range(BLOCK_ROWS):
        slot.append(total)
        total = total + has[i]
    row = jnp.zeros((1, 128), jnp.int32)
    filled = jnp.zeros((1, 128), jnp.int32)
    for i in range(BLOCK_ROWS):
        hit = jnp.where(lax.shift_right_logical(lane, 3) == slot[i], has[i], 0)
        row = row + i * hit
        filled = filled + hit
    tab_v[TAB_C : TAB_C + 1] = jnp.where(filled > 0, rel(row * PARTS + (lane & 7)), ZERO_TILE)

    def find(q, carry):
        source, mine = carry
        reader = readers[q]
        return jnp.where(dest == reader, q, source), jnp.where(reader == p, q, mine)

    source, mine = lax.fori_loop(0, N_REP, find, (jnp.zeros((1, 128), jnp.int32), nil))
    source_row = lax.shift_right_logical(source, 3)
    place = jnp.zeros((1, 128), jnp.int32)
    for i in range(BLOCK_ROWS):
        place = place + jnp.where(source_row == i, has[i] * (slot[i] + 1), 0)
    found = jnp.where(place > 0, (place - 1) * PARTS + (source & 7), ZERO_RESULT)
    tab_v[TAB_D : TAB_D + 1] = jnp.minimum(found, ZERO_RESULT)
    mine_row = lax.div(mine, PARTS)
    holder = jnp.zeros((1, 128), jnp.int32)
    for j in range(COLS):
        holder = jnp.where(lane == j, owners[mine_row, j], holder)
    tab_v[TAB_E : TAB_E + 1] = rel(holder)


def hand_over(upd_in, left_in, right_in, upd_out, left_out, right_out):
    upd_out[...] = upd_in[...]
    left_out[...] = left_in[...]
    right_out[...] = right_in[...]


def on_device(grad_part, owners, readers, left_stat, right_stat, left_root, right_root):
    grads = jnp.transpose(grad_part[0], (1, 0, 2))
    strips = jnp.transpose(right_root[0], (0, 2, 1))
    hbm = pl.BlockSpec(memory_space=pl.ANY)
    vmem = pl.BlockSpec(memory_space=pltpu.VMEM)
    dma = pltpu.SemaphoreType.DMA
    update, left_next, right_next = pl.pallas_call(
        kernel,
        out_shape=(
            jax.ShapeDtypeStruct((COLS, 32, 64), bf16),
            jax.ShapeDtypeStruct(left_stat.shape, f32),
            jax.ShapeDtypeStruct(right_stat.shape, f32),
        ),
        in_specs=[pl.BlockSpec(memory_space=pltpu.SMEM)] * 2 + [hbm] * 5,
        out_specs=(hbm, hbm, hbm),
        scratch_shapes=[
            pltpu.VMEM((2, COLS, 16, 512), f32),
            pltpu.VMEM((NY, COLS, 16, 128), f32),
            pltpu.VMEM((2, 4, COLS, 16, 128), bf16),
            pltpu.VMEM((2, 4, COLS, 16, 128), bf16),
            pltpu.VMEM((COLS + 1, 16, 128), bf16),
            pltpu.VMEM((N_REP, 16, 128), bf16),
            pltpu.VMEM((N_REP + 1, 16, 128), bf16),
            pltpu.VMEM((SLOTS, 4, 4, PARTS, 16, 128), bf16),
            pltpu.VMEM((SLOTS * PARTS + 1, 16, 128), bf16),
            pltpu.VMEM((N_REP, 16, 128), bf16),
            pltpu.VMEM((N_REP, 16, 128), bf16),
            pltpu.VMEM((SLOTS, 32, 512), f32),
            pltpu.VMEM((SLOTS, 32, 512), f32),
            pltpu.VMEM((SLOTS, 512, 512), bf16),
            pltpu.VMEM((SLOTS, 32, 512), bf16),
            pltpu.VMEM((SLOTS, 32, 512), f32),
            pltpu.VMEM((SLOTS, 32, 512), f32),
            pltpu.VMEM((COLS, 32, 64), bf16),
            pltpu.VMEM((4, 128), jnp.int32),
            pltpu.SMEM((4, 128), jnp.int32),
            dma((4,)), dma((4,)), dma((1,)), dma((NY,)), dma((NY,)), dma((32,)), dma((32,)), dma((2,)),
            dma((8 * SLOTS,)), dma((8 * SLOTS,)), dma((9 * SLOTS,)), dma((9 * SLOTS,)), dma((2,)),
            pltpu.SemaphoreType.REGULAR((5,)), dma((2 * SLOTS + 1,)),
        ],
        compiler_params=pltpu.CompilerParams(
            collective_id=0, has_side_effects=True, vmem_limit_bytes=60 * 1024 * 1024
        ),
        cost_estimate=pl.CostEstimate(flops=300_000_000, bytes_accessed=8_000_000, transcendentals=0),
    )(owners, readers, grads, left_stat, right_stat, left_root, strips)
    update, left_next, right_next = pl.pallas_call(
        hand_over,
        out_shape=tuple(jax.ShapeDtypeStruct(one.shape, one.dtype) for one in (update, left_next, right_next)),
        in_specs=[vmem] * 3,
        out_specs=(vmem,) * 3,
        compiler_params=pltpu.CompilerParams(vmem_limit_bytes=60 * 1024 * 1024),
    )(update, left_next, right_next)
    return jnp.transpose(update, (2, 0, 1)), left_next, right_next


def solution(mesh):
    placed = (
        P("grp", "rep", None, None),
        P(),
        P(),
        P("rep", None, "grp", None),
        P("rep", None, "grp", None),
        P("rep", None, None, None),
        P("rep", None, None, "grp"),
    )
    return jax.shard_map(
        on_device,
        mesh=mesh,
        in_specs=placed,
        out_specs=(P("rep", None, "grp"), P("rep", None, "grp", None), P("rep", None, "grp", None)),
        check_vma=False,
    )
```

time: 102 us -> 74.8 us (0.73)
  Pallas kernels: 83.7 us -> 73.8 us
  local copies, waits for them, and re-layouts: 9.79 us -> 0 us
  other arithmetic: 4.49 us -> 0 us
  between operations: 3.38 us -> 0.64 us
    pallas_call x1 -> x2, Pallas kernels: 83.7 us -> 73.8 us  [the longest x1 71.8 us: on_device(): pl.pallas_call(kernel, out_shape=(jax.ShapeDtypeStruct((COLS, 32, 64), bf...]
    unnamed x9 -> x0, local copies, waits for them, and re-layouts: 6.53 us -> none
    select_n x3 -> x0, other arithmetic: 1.33 us -> none  [the longest x1 1.3 us: tables(): jnp.where(place > 0, (place - 1) * PARTS + source % PARTS, ZERO_RESULT)]
    another operation x2 -> x0, local copies, waits for them, and re-layouts: 1.23 us -> none  [on_device(): strips = jnp.tile(right_root[0], (1, 1, 4))]
    reduce_sum x4 -> x0, other arithmetic: 1.16 us -> none  [the longest x1 0.83 us: tables(): jnp.sum(jnp.where(readers[None, :] == dest[:, None], n[None, :], 0), axis=1)]
where the time goes in v2:
time: 74.8 us; the launch traced here: 74.4 us
  Pallas kernels  73.8 us (99%)
    pallas_call x1, Pallas kernels, on_device(): pl.pallas_call(kernel, out_shape=(jax.ShapeDtypeStruct((COLS, 32, 64), bf...  71.8 us
    pallas_call x1, Pallas kernels, on_device(): pl.pallas_call(hand_over, out_shape=tuple((jax.ShapeDtypeStruct(one.shape...  2 us

profile of v2, /device:TPU:1, one launch (start us, length us, event | category | flops | bytes accessed | tf_op | source)
XLA Modules:
  0.0 74.4 jit_solution(7579113566438319110)
XLA Ops:
  0.6 71.8 %shard_map.94 = (bf16[20,32,64]{2,1,0:T(8,128)(2,1)}, f32[1,4,32,512]{3,2,1,0:T(8,128)}, f32[1,4,32,512]{3,2,1,0:T(8,128)}) custom-call(s32[6,20]{1,0:T(8,128)} %owners.1, s32[48]{0:T(128)} %readers.1, f32[20,64,512]{2,1,0:T(8,128)} %bitcast.7, f32[1,4,32,512]{3,2,1,0:T(8,128)} %lstat_hbm.1, f32[1,4,32,512]{3,2,1,0:T(8,128)} %rstat_hbm.1, ...), custom_call_target="tpu_custom_call" | custom-call | flops 300000000 | bytes 8000000 | tf_op jit(solution)/shard_map/pallas_call | solution.py:418
  72.4 2.0 %shard_map.95 = (bf16[20,32,64]{2,1,0:T(8,128)(2,1)}, f32[1,4,32,512]{3,2,1,0:T(8,128)}, f32[1,4,32,512]{3,2,1,0:T(8,128)}) custom-call(bf16[20,32,64]{2,1,0:T(8,128)(2,1)} %get-tuple-element.9.upd_in, f32[1,4,32,512]{3,2,1,0:T(8,128)} %get-tuple-element.10.left_in, f32[1,4,32,512]{3,2,1,0:T(8,128)} %get-tuple-element.11.right_in), custom_call_target="tpu_custom_call" | custom-call | tf_op jit(solution)/shard_map/pallas_call | solution.py:457

commit v3 on v2

--- a/solution.py
+++ b/solution.py
@@ -45,11 +45,18 @@
     sibling = g + 1 - 2 * core
     up = lax.rem(y + 1, NY) * 2 + core
     down = lax.rem(y + NY - 1, NY) * 2 + core
+    up_two = lax.rem(y + 2, NY) * 2 + core
+    down_two = lax.rem(y + NY - 2, NY) * 2 + core
     at_x = [lax.rem(px + dx, NX) * NZ for dx in range(NX)]
     at_z = [lax.rem(pz + dz, NZ) for dz in range(NZ)]
 
     def peer(dx, dz):
         return at_x[dx % NX] + at_z[dz % NZ]
+
+    def along(way, dist):
+        if dist == 4:
+            return down_two if way else up_two
+        return down if way else up
 
     def remote(src, dst, ssem, rsem, grp, rep):
         return pltpu.make_async_remote_copy(
@@ -82,7 +89,7 @@
         one.start()
 
     barrier = pltpu.get_barrier_semaphore()
-    for who in (sibling, up, down):
+    for who in (sibling, up, down, up_two, down_two):
         pl.semaphore_signal(barrier, inc=1, device_id=(who, p), device_id_type=MESH)
 
     for dx, dz in ((1, 0), (-1, 0), (0, 1), (0, -1)):
@@ -90,7 +97,7 @@
     tiles[ZERO_PIECE] = jnp.zeros((16, 128), bf16)
     recv_b[ZERO_TILE] = jnp.zeros((16, 128), bf16)
     res[ZERO_RESULT] = jnp.zeros((16, 128), bf16)
-    pl.semaphore_wait(barrier, 7)
+    pl.semaphore_wait(barrier, 9)
 
     rounds = (
         ((0, 1), (0, -1)), ((0, 2), (0, -2)), ((0, 2), (0, -2)), ((1, 0), (-1, 0)), ((1, 0),),
@@ -107,6 +114,62 @@
 
     strip_of(4).start()
     tell(0)
+    strip_of(3).start()
+    strip_of(5).start()
+    hear(0)
+    for one in own_loads:
+        one.wait()
+
+    def pair_sum(k, j):
+        there = lax.rem(y + k, NY)
+        at = (lax.div(there, 4), j, slice(None), pl.ds(pl.multiple_of(lax.rem(there, 4) * 128, 128), 128))
+        return own[at] + sib[k, j]
+
+    arrived = set()
+
+    def need(k):
+        if k not in arrived:
+            arrived.add(k)
+            strip_of(k).wait_recv()
+
+    def chain(way, dist, part):
+        slot = (way * 4 + dist - 1) * 4 + part
+        span = pl.ds(part * QUARTER, QUARTER)
+        return remote(
+            send_a.at[way, dist - 1, span], recv_a.at[way, dist - 1, span],
+            a_ssem.at[slot], a_rsem.at[slot], along(way, dist), p,
+        )
+
+    def span_of(part):
+        return range(part * QUARTER, part * QUARTER + QUARTER)
+
+    def send_sum(way, dist, part, sources):
+        k = NY - dist if way else dist
+        need(k)
+        for source in sources:
+            chain(way, source, part).wait_recv()
+        for j in span_of(part):
+            total = pair_sum(k, j)
+            for source in sources:
+                total = total + recv_a[way, source - 1, j].astype(f32)
+            send_a[way, dist - 1, j] = total.astype(bf16)
+        chain(way, dist, part).start()
+
+    far_parts = ((0, 1), (2, 3))
+    for i in range(2):
+        for way in range(2):
+            send_sum(way, 4, far_parts[way][i], ())
+    strip_of(2).start()
+    strip_of(6).start()
+    fill_tables(owners, readers, tab_v, p, px, pz)
+    tab_copy = pltpu.make_async_copy(tab_v, tab, tab_sem.at[0])
+    tab_copy.start()
+    hear(1)
+    for i in range(2):
+        for way in range(2):
+            send_sum(way, 3, far_parts[1 - way][i], ())
+    for k in (1, 7, 0):
+        strip_of(k).start()
     late_loads = [
         pltpu.make_async_copy(src, dst, load_sem.at[i])
         for i, (src, dst) in enumerate(
@@ -115,71 +178,17 @@
     ]
     for one in late_loads:
         one.start()
-    fill_tables(owners, readers, tab_v, p, px, pz)
-    tab_copy = pltpu.make_async_copy(tab_v, tab, tab_sem.at[0])
-    tab_copy.start()
-    strip_of(3).start()
-    strip_of(5).start()
-    hear(0)
-    for one in own_loads:
-        one.wait()
-
-    def pair_sum(k, j):
-        there = lax.rem(y + k, NY)
-        at = (lax.div(there, 4), j, slice(None), pl.ds(pl.multiple_of(lax.rem(there, 4) * 128, 128), 128))
-        return own[at] + sib[k, j]
-
-    arrived = set()
-
-    def need(k):
-        if k not in arrived:
-            arrived.add(k)
-            strip_of(k).wait_recv()
-
-    def chain(way, dist, part):
-        slot = (way * 4 + dist - 1) * 4 + part
-        span = pl.ds(part * QUARTER, QUARTER)
-        return remote(
-            send_a.at[way, dist - 1, span], recv_a.at[way, dist - 1, span],
-            a_ssem.at[slot], a_rsem.at[slot], down if way else up, p,
-        )
-
-    def span_of(part):
-        return range(part * QUARTER, part * QUARTER + QUARTER)
-
-    def send_sum(way, dist, part, from_dist):
-        k = NY - dist if way else dist
-        need(k)
-        if from_dist:
-            chain(way, from_dist, part).wait_recv()
-        for j in span_of(part):
-            total = pair_sum(k, j)
-            if from_dist:
-                total = total + recv_a[way, from_dist - 1, j].astype(f32)
-            send_a[way, dist - 1, j] = total.astype(bf16)
-        chain(way, dist, part).start()
-
-    far_parts = ((0, 1), (2, 3))
-    for i in range(2):
-        for way in range(2):
-            send_sum(way, 4, far_parts[way][i], None)
-    strip_of(2).start()
-    strip_of(6).start()
-    hear(1)
-    for i in range(2):
-        for way in range(2):
-            send_sum(way, 3, far_parts[1 - way][i], None)
-    for k in (1, 7, 0):
-        strip_of(k).start()
     hear(2)
     for i in range(2):
         for way in range(2):
-            send_sum(way, 3, far_parts[way][i], 4)
+            send_sum(way, 3, far_parts[way][i], ())
     for dist in (2, 1):
         hear(5 - dist)
         for i in range(4):
             for way in range(2):
-                send_sum(way, dist, (2, 3, 0, 1)[i] if way == 0 else i, dist + 1)
+                part = (2, 3, 0, 1)[i] if way == 0 else i
+                far = (4,) if dist == 2 and part in far_parts[way] else ()
+                send_sum(way, dist, part, (dist + 1,) + far)
     need(0)
     for part in range(4):
         for way in range(2):
@@ -208,7 +217,7 @@
     def ring(way, dist, s, y_of):
         place = home(y_of, core, s)
         index = (way * 4 + dist - 1) * SLOTS + s
-        return remote(place, place, c_ssem.at[index], c_rsem.at[index], down if way else up, p)
+        return remote(place, place, c_ssem.at[index], c_rsem.at[index], along(way, dist), p)
 
     def across(index, s, y_of, core_of):
         place = home(y_of, core_of, s)
@@ -233,14 +242,18 @@
             if carries(way, dist, s):
                 origin = back(way, dist)
                 ring(way, dist, s, origin).wait_recv()
-                if dist < 4 and carries(way, dist + 1, s):
+                if dist == 2 and carries(way, 4, s):
+                    ring(way, 4, s, origin).start()
+                if dist < 3:
                     ring(way, dist + 1, s, origin).start()
                 across(relay(way, dist), s, origin, core).start()
 
-    def gathered(s):
-        across(0, s, y, 1 - core).wait_recv()
-        for way in range(2):
-            for dist in range(1, 5):
+    def sibling_pieces(dist):
+        for s in range(SLOTS):
+            if dist == 0:
+                across(0, s, y, 1 - core).wait_recv()
+                continue
+            for way in range(2):
                 if carries(way, dist, s):
                     across(relay(way, dist), s, back(way, dist), 1 - core).wait_recv()
 
@@ -261,21 +274,16 @@
             res[s * PARTS + 2 * v] = jnp.where(left_half, top, pltpu.roll(low, 64, 1)).astype(bf16)
             res[s * PARTS + 2 * v + 1] = jnp.where(left_half, pltpu.roll(top, 64, 1), low).astype(bf16)
 
-    groups = ((0, 1), (2, 3))
-    for s in groups[0]:
+    for s in range(SLOTS):
         launch(s)
     for one in late_loads:
         one.wait()
-    for s in groups[0]:
-        for way in range(2):
-            ring(way, 1, s, y).wait_send()
-    for s in groups[1]:
-        launch(s)
     for dist in range(1, 5):
         for s in range(SLOTS):
             forward(dist, s)
+        sibling_pieces(dist - 1)
+    sibling_pieces(4)
     for s in range(SLOTS):
-        gathered(s)
         precondition(s)
 
     recv_d[0] = res[tab[TAB_D, 0]]
@@ -309,18 +317,6 @@
         rout[s] = decay * rstat[s] + (1.0 - decay) * second
         out_right(s).start()
 
-    all_d.wait_recv()
-
-    def unpack(j, carry):
-        rows = recv_d[tab[TAB_E, j]]
-        upd[j, 0:16] = rows[:, 0:64]
-        upd[j, 16:32] = pltpu.roll(rows.astype(f32), 64, 1)[:, 0:64].astype(bf16)
-        return carry
-
-    lax.fori_loop(0, COLS, unpack, 0, unroll=4)
-    out_update = out_copy(upd, upd_hbm, 2 * SLOTS)
-    out_update.start()
-
     for k in range(NY):
         strip_of(k).wait_send()
     for way in range(2):
@@ -334,13 +330,21 @@
         for way in range(2):
             for dist in range(1, 5):
                 if carries(way, dist, s):
-                    if dist > 1 or s in groups[1]:
-                        ring(way, dist, s, y).wait_send()
+                    ring(way, dist, s, y).wait_send()
                     across(relay(way, dist), s, y, core).wait_send()
-    all_d.wait_send()
     for s in range(SLOTS):
         out_left(s).wait()
         out_right(s).wait()
+    all_d.wait_recv()
+
+    for j in range(COLS):
+        rows = recv_d[tab[TAB_E, j]]
+        upd[j, 0:16] = rows[:, 0:64]
+        upd[j, 16:32] = pltpu.roll(rows.astype(f32), 64, 1)[:, 0:64].astype(bf16)
+    out_update = out_copy(upd, upd_hbm, 2 * SLOTS)
+    out_update.start()
+
+    all_d.wait_send()
     out_update.wait()
 
 
@@ -403,17 +407,28 @@
     tab_v[TAB_E : TAB_E + 1] = rel(holder)
 
 
-def hand_over(upd_in, left_in, right_in, upd_out, left_out, right_out):
-    upd_out[...] = upd_in[...]
-    left_out[...] = left_in[...]
-    right_out[...] = right_in[...]
+def hand_over(left_in, right_in, upd_in, left_out, right_out, upd_out, left, right, upd, in_sem, out_sem):
+    steps = []
+    for src, mid, dst in ((left_in, left, left_out), (right_in, right, right_out)):
+        for half in range(2):
+            at = (0, pl.ds(half * 2, 2))
+            steps.append((src.at[at], mid.at[at], dst.at[at]))
+    steps.append((upd_in, upd, upd_out))
+    into = [pltpu.make_async_copy(src, mid, in_sem.at[i]) for i, (src, mid, _) in enumerate(steps)]
+    out = [pltpu.make_async_copy(mid, dst, out_sem.at[i]) for i, (_, mid, dst) in enumerate(steps)]
+    for one in into:
+        one.start()
+    for here, there in zip(into, out):
+        here.wait()
+        there.start()
+    for one in out:
+        one.wait()
 
 
 def on_device(grad_part, owners, readers, left_stat, right_stat, left_root, right_root):
     grads = jnp.transpose(grad_part[0], (1, 0, 2))
     strips = jnp.transpose(right_root[0], (0, 2, 1))
     hbm = pl.BlockSpec(memory_space=pl.ANY)
-    vmem = pl.BlockSpec(memory_space=pltpu.VMEM)
     dma = pltpu.SemaphoreType.DMA
     update, left_next, right_next = pl.pallas_call(
         kernel,
@@ -454,13 +469,15 @@
         ),
         cost_estimate=pl.CostEstimate(flops=300_000_000, bytes_accessed=8_000_000, transcendentals=0),
     )(owners, readers, grads, left_stat, right_stat, left_root, strips)
-    update, left_next, right_next = pl.pallas_call(
+    results = (left_next, right_next, update)
+    left_next, right_next, update = pl.pallas_call(
         hand_over,
-        out_shape=tuple(jax.ShapeDtypeStruct(one.shape, one.dtype) for one in (update, left_next, right_next)),
-        in_specs=[vmem] * 3,
-        out_specs=(vmem,) * 3,
+        out_shape=tuple(jax.ShapeDtypeStruct(one.shape, one.dtype) for one in results),
+        in_specs=[hbm] * 3,
+        out_specs=(hbm,) * 3,
+        scratch_shapes=[pltpu.VMEM(one.shape, one.dtype) for one in results] + [dma((5,)), dma((5,))],
         compiler_params=pltpu.CompilerParams(vmem_limit_bytes=60 * 1024 * 1024),
-    )(update, left_next, right_next)
+    )(*results)
     return jnp.transpose(update, (2, 0, 1)), left_next, right_next
 
 

time: 74.8 us -> 72.9 us (0.975)
  Pallas kernels: 73.8 us -> 72.1 us
    pallas_call x1, Pallas kernels: 71.8 us -> 70.2 us  [on_device(): pl.pallas_call(kernel, out_shape=(jax.ShapeDtypeStruct((COLS, 32, 64), bf...]
where the time goes in v3:
time: 72.9 us; the launch traced here: 72.7 us
  Pallas kernels  72.1 us (99%)
    pallas_call x1, Pallas kernels, on_device(): pl.pallas_call(kernel, out_shape=(jax.ShapeDtypeStruct((COLS, 32, 64), bf...  70.2 us
    pallas_call x1, Pallas kernels, on_device(): pl.pallas_call(hand_over, out_shape=tuple((jax.ShapeDtypeStruct(one.shape...  1.93 us

profile of v3, /device:TPU:1, one launch (start us, length us, event | category | flops | bytes accessed | tf_op | source)
XLA Modules:
  0.0 72.7 jit_solution(1773685870600678817)
XLA Ops:
  0.6 70.2 %shard_map.94 = (bf16[20,32,64]{2,1,0:T(8,128)(2,1)}, f32[1,4,32,512]{3,2,1,0:T(8,128)}, f32[1,4,32,512]{3,2,1,0:T(8,128)}) custom-call(s32[6,20]{1,0:T(8,128)} %owners.1, s32[48]{0:T(128)} %readers.1, f32[20,64,512]{2,1,0:T(8,128)} %bitcast.7, f32[1,4,32,512]{3,2,1,0:T(8,128)} %lstat_hbm.1, f32[1,4,32,512]{3,2,1,0:T(8,128)} %rstat_hbm.1, ...), custom_call_target="tpu_custom_call" | custom-call | flops 300000000 | bytes 8000000 | tf_op jit(solution)/shard_map/pallas_call | solution.py:433
  70.8 1.9 %shard_map.95 = (f32[1,4,32,512]{3,2,1,0:T(8,128)}, f32[1,4,32,512]{3,2,1,0:T(8,128)}, bf16[20,32,64]{2,1,0:T(8,128)(2,1)}) custom-call(f32[1,4,32,512]{3,2,1,0:T(8,128)} %get-tuple-element.9.left_in, f32[1,4,32,512]{3,2,1,0:T(8,128)} %get-tuple-element.10.right_in, bf16[20,32,64]{2,1,0:T(8,128)(2,1)} %get-tuple-element.11.upd_in), custom_call_target="tpu_custom_call" | custom-call | tf_op jit(solution)/shard_map/pallas_call | solution.py:473
